TPU v7x, 32 devices: a whole 2x2x4 slice. The times are simulated.
32 devices in a mesh: batch: 8 (over z, y), seq: 4 (over x, core).
Axes of the slice: x: 2, y: 2, z: 4, core: 2. Of those that a mesh axis runs over, the one named last changes fastest.
Arguments:
- layer_activations: bfloat16 [8, 4096, 512], P('batch', 'seq'), may hold values from -6 to 6
- sequence_extents: int32 [8], P('batch'), may hold values from 3073 to 4096, as said below
- position_cluster_label: int32 [8, 4096], P('batch', 'seq'), may hold values from 0 to 31, as said below
- cluster_sharpness: float32 [1], replicated, may hold values from 0.7 to 1.4
- heed_scale_factor: bfloat16 [512], replicated, may hold values from 0.5 to 1.5
- triple_entry_matrix: bfloat16 [512, 1536], replicated, may hold values from -0.25 to 0.25
- heed_exit_matrix: bfloat16 [512, 512], replicated, may hold values from -6 to 6
- blend_scale_factor: bfloat16 [512], replicated, may hold values from 0.5 to 1.5
- router_matrix: bfloat16 [512, 2], replicated, may hold values from -0.25 to 0.25
- specialist_entry_matrix: bfloat16 [2, 512, 2048], replicated, may hold values from -1 to 1
- specialist_exit_matrix: bfloat16 [2, 2048, 512], replicated, may hold values from -2 to 2
- upstream_derivative: bfloat16 [8, 4096, 512], P('batch', 'seq'), may hold values from -6 to 6
Outputs:
- block_out: bfloat16 [8, 4096, 512], P('batch', 'seq')
- tokens_grad: bfloat16 [8, 4096, 512], P('batch', 'seq')
- grad_gain_attn: float32 [512], replicated
- grad_qkv: float32 [512, 1536], replicated
- grad_out: float32 [512, 512], replicated
- grad_gain_mix: float32 [512], replicated
- grad_ctrl: float32 [512, 2], replicated
- grad_in: float32 [2, 512, 2048], replicated
- grad_down: float32 [2, 2048, 512], replicated
Inputs may be any that keep to these rules, and one draw needn't show every extreme that they name: `sequence_extents`: one sequence has length 4096 in every draw. `position_cluster_label`: within the 1 x 1024 positions that share a batch index and a seq index, every value is held by exactly 32 positions, in no causal order.
All inputs are finite; a program needn't handle non-finite values.
Results may differ from a plain program's by a relative error of at most 0.024.
Values may be sent and summed in bfloat16 or wider, within the bound.
No kernel may reach another device: no remote copies, remote signals or barrier semaphores. Data moves between devices by JAX's collectives and lax.ppermute only.
A program may use at most 256 MiB of HBM per device.

v0:
```python
import jax
import jax.numpy as jnp
from jax import lax
from jax.sharding import PartitionSpec as P

HEADS = 8
HEAD = 64
GROUP = 32


EPSILON = 1e-06
MASKED = -1e30


def rms_norm(values, gain):
    inverse = lax.rsqrt(jnp.mean(values * values, axis=-1, keepdims=True) + EPSILON)
    return values * inverse * gain


def gelu_exact(values):
    return jax.nn.gelu(values, approximate=False)


def cluster_blend_shares(logit_vals, cluster_assignment):
    spread_mask = cluster_assignment[:, :, None]
    masked_vals = jnp.where(spread_mask, logit_vals[None, :, :], -jnp.inf)
    group_peak = jnp.max(masked_vals, axis=1)
    token_peak = jnp.sum(jnp.where(spread_mask, group_peak[:, None, :], 0.0), axis=0)
    raised = jnp.exp(logit_vals - token_peak)
    group_total = jnp.sum(jnp.where(spread_mask, raised[None, :, :], 0.0), axis=1)
    token_total = jnp.sum(jnp.where(spread_mask, group_total[:, None, :], 0.0), axis=0)
    return raised / token_total


def split_heads(stacked):
    seq_count = stacked.shape[0]
    length = stacked.shape[1]
    return (
        stacked.reshape(seq_count, length, HEADS, HEAD)
        .transpose(0, 2, 1, 3)
        .reshape(seq_count * HEADS, length, HEAD)
    )


def merge_heads(stacked, seq_count):
    length = stacked.shape[1]
    head_dim = stacked.shape[2]
    return (
        stacked.reshape(seq_count, HEADS, length, head_dim)
        .transpose(0, 2, 1, 3)
        .reshape(seq_count * length, HEADS * head_dim)
    )


def head_probs(query_head, key_head, limit_len, query_pos, key_pos, score_scale):
    raw_scores = (
        jnp.einsum("qd,kd->qk", query_head, key_head, preferred_element_type=jnp.float32)
        * score_scale
    )
    allowed = (key_pos[None, :] <= query_pos[:, None]) & (key_pos[None, :] < limit_len)
    return jnp.where(allowed, raw_scores, MASKED)


def attend_head(query_head, key_head, value_head, limit_len, query_pos, key_pos, score_scale):
    scores = head_probs(query_head, key_head, limit_len, query_pos, key_pos, score_scale)
    row_peak = jnp.max(scores, axis=1)
    raised = jnp.exp(scores - row_peak[:, None])
    row_total = jnp.sum(raised, axis=1)
    attn_probs = raised / row_total[:, None]
    attended = jnp.einsum(
        "qk,kd->qd", attn_probs.astype(jnp.bfloat16), value_head, preferred_element_type=jnp.float32
    )
    return (attended, row_peak, row_total)


def attend_back(
    query_head,
    key_head,
    value_head,
    grad_head,
    row_peak,
    row_total,
    limit_len,
    query_pos,
    key_pos,
    score_scale,
):
    scores = head_probs(query_head, key_head, limit_len, query_pos, key_pos, score_scale)
    attn_probs = jnp.exp(scores - row_peak[:, None]) / row_total[:, None]
    probs_low = attn_probs.astype(jnp.bfloat16)
    back_probs = jnp.einsum("qd,kd->qk", grad_head, value_head, preferred_element_type=jnp.float32)
    row_inner = jnp.sum(attn_probs * back_probs, axis=1)
    back_scores = (attn_probs * (back_probs - row_inner[:, None])).astype(jnp.bfloat16)
    back_query = (
        jnp.einsum("qk,kd->qd", back_scores, key_head, preferred_element_type=jnp.float32)
        * score_scale
    )
    back_keys = (
        jnp.einsum("qk,qd->kd", back_scores, query_head, preferred_element_type=jnp.float32)
        * score_scale
    )
    back_values = jnp.einsum("qk,qd->kd", probs_low, grad_head, preferred_element_type=jnp.float32)
    return (back_query, jnp.concatenate([back_keys, back_values], axis=1))


def body(
    layer_activations,
    sequence_extents,
    position_cluster_label,
    cluster_sharpness,
    heed_scale_factor,
    triple_entry_matrix,
    heed_exit_matrix,
    blend_scale_factor,
    router_matrix,
    specialist_entry_matrix,
    specialist_exit_matrix,
    upstream_derivative,
):
    seq_count, pos_count, model_width = layer_activations.shape
    tok_count = seq_count * pos_count
    full_len = pos_count * lax.axis_size("seq")
    groups = tok_count // GROUP
    score_scale = HEAD ** (-0.5)
    query_pos = lax.axis_index("seq") * pos_count + jnp.arange(pos_count, dtype=jnp.int32)
    key_pos = jnp.arange(full_len, dtype=jnp.int32)
    limits = jnp.repeat(sequence_extents, HEADS)
    flat_rows = layer_activations.reshape(tok_count, model_width).astype(jnp.float32)
    normed_attn, norm_attn_back = jax.vjp(
        rms_norm, flat_rows, heed_scale_factor.astype(jnp.float32)
    )
    normed_low = normed_attn.astype(jnp.bfloat16)
    qkv_low = jnp.dot(normed_low, triple_entry_matrix, preferred_element_type=jnp.float32).astype(
        jnp.bfloat16
    )
    query_part = qkv_low[:, :model_width].reshape(seq_count, pos_count, model_width)
    key_part = qkv_low[:, model_width : 2 * model_width].reshape(seq_count, pos_count, model_width)
    value_part = qkv_low[:, 2 * model_width :].reshape(seq_count, pos_count, model_width)
    whole_keys, whole_values = (
        lax.all_gather(key_part, "seq", axis=1, tiled=True),
        lax.all_gather(value_part, "seq", axis=1, tiled=True),
    )
    query_items = split_heads(query_part)
    key_items = split_heads(whole_keys)
    value_items = split_heads(whole_values)

    def forward_item(pieces):
        query_head, key_head, value_head, limit_len = pieces
        return attend_head(
            query_head, key_head, value_head, limit_len, query_pos, key_pos, score_scale
        )

    head_out, row_peak, row_total = lax.map(
        forward_item, (query_items, key_items, value_items, limits)
    )
    attended_low = merge_heads(head_out, seq_count).astype(jnp.bfloat16)
    branch = jnp.dot(attended_low, heed_exit_matrix, preferred_element_type=jnp.float32)
    resid = flat_rows + branch
    mix_normed, norm_mix_back = jax.vjp(rms_norm, resid, blend_scale_factor.astype(jnp.float32))
    mix_low = mix_normed.astype(jnp.bfloat16)
    logit_vals = jnp.dot(mix_low, router_matrix, preferred_element_type=jnp.float32)
    cluster_assignment = (
        position_cluster_label.reshape(tok_count)[None, :]
        == jnp.arange(groups, dtype=jnp.int32)[:, None]
    )

    def weigh(router_scores):
        return cluster_blend_shares(router_scores / cluster_sharpness[0], cluster_assignment)

    blend_coefficients, weigh_back = jax.vjp(weigh, logit_vals)
    weight_low = blend_coefficients.astype(jnp.bfloat16)
    mixing = jnp.where(
        cluster_assignment[None, :, :], weight_low.T[:, None, :], jnp.zeros((), jnp.bfloat16)
    )
    mixed_low = jnp.einsum(
        "egt,td->egd", mixing, mix_low, preferred_element_type=jnp.float32
    ).astype(jnp.bfloat16)
    inner = jnp.einsum(
        "egd,edh->egh", mixed_low, specialist_entry_matrix, preferred_element_type=jnp.float32
    )
    active, gelu_back = jax.vjp(gelu_exact, inner)
    active_low = active.astype(jnp.bfloat16)
    expert_low = jnp.einsum(
        "egh,ehd->egd", active_low, specialist_exit_matrix, preferred_element_type=jnp.float32
    ).astype(jnp.bfloat16)
    spread = jnp.einsum("egt,egd->td", mixing, expert_low, preferred_element_type=jnp.float32)
    block_out = (resid + spread).astype(jnp.bfloat16).reshape(layer_activations.shape)
    cot_low = upstream_derivative.reshape(tok_count, model_width)
    cot_full = cot_low.astype(jnp.float32)
    back_expert = jnp.einsum(
        "egt,td->egd", mixing, cot_low, preferred_element_type=jnp.float32
    ).astype(jnp.bfloat16)
    grad_down = jnp.einsum(
        "egh,egd->ehd", active_low, back_expert, preferred_element_type=jnp.float32
    )
    back_active = jnp.einsum(
        "egd,ehd->egh", back_expert, specialist_exit_matrix, preferred_element_type=jnp.float32
    )
    back_inner = gelu_back(back_active)[0].astype(jnp.bfloat16)
    grad_in = jnp.einsum("egd,egh->edh", mixed_low, back_inner, preferred_element_type=jnp.float32)
    back_mixed = jnp.einsum(
        "egh,edh->egd", back_inner, specialist_entry_matrix, preferred_element_type=jnp.float32
    ).astype(jnp.bfloat16)
    back_mixing = jnp.einsum("td,egd->egt", cot_low, expert_low, preferred_element_type=jnp.float32)
    back_mixing = back_mixing + jnp.einsum(
        "td,egd->egt", mix_low, back_mixed, preferred_element_type=jnp.float32
    )
    back_weight = jnp.sum(jnp.where(cluster_assignment[None, :, :], back_mixing, 0.0), axis=1).T
    back_logits = weigh_back(back_weight)[0].astype(jnp.bfloat16)
    grad_ctrl = jnp.einsum("td,te->de", mix_low, back_logits, preferred_element_type=jnp.float32)
    back_mix = jnp.einsum("egt,egd->td", mixing, back_mixed, preferred_element_type=jnp.float32)
    back_mix = back_mix + jnp.einsum(
        "te,de->td", back_logits, router_matrix, preferred_element_type=jnp.float32
    )
    back_resid_norm, grad_gain_mix = norm_mix_back(back_mix)
    back_resid = cot_full + back_resid_norm
    back_branch = back_resid.astype(jnp.bfloat16)
    grad_out = jnp.einsum(
        "td,te->de", attended_low, back_branch, preferred_element_type=jnp.float32
    )
    back_attended = jnp.einsum(
        "te,de->td", back_branch, heed_exit_matrix, preferred_element_type=jnp.float32
    ).astype(jnp.bfloat16)
    grad_items = split_heads(back_attended.reshape(seq_count, pos_count, model_width))

    def backward_item(pieces):
        query_head, key_head, value_head, grad_head, peak_item, total_item, limit_len = pieces
        return attend_back(
            query_head,
            key_head,
            value_head,
            grad_head,
            peak_item,
            total_item,
            limit_len,
            query_pos,
            key_pos,
            score_scale,
        )

    query_grads, pair_grads = lax.map(
        backward_item,
        (query_items, key_items, value_items, grad_items, row_peak, row_total, limits),
    )
    pair_grads = pair_grads.reshape(seq_count, HEADS, full_len, 2 * HEAD)
    own_pairs = lax.psum_scatter(pair_grads, "seq", scatter_dimension=2, tiled=True)
    own_pairs = own_pairs.reshape(seq_count * HEADS, pos_count, 2 * HEAD)
    back_query = merge_heads(query_grads, seq_count).astype(jnp.bfloat16)
    back_keys = merge_heads(own_pairs[:, :, :HEAD], seq_count).astype(jnp.bfloat16)
    back_values = merge_heads(own_pairs[:, :, HEAD:], seq_count).astype(jnp.bfloat16)
    back_qkv = jnp.concatenate([back_query, back_keys, back_values], axis=1)
    grad_qkv = jnp.einsum("td,tf->df", normed_low, back_qkv, preferred_element_type=jnp.float32)
    back_normed = jnp.einsum(
        "tf,df->td", back_qkv, triple_entry_matrix, preferred_element_type=jnp.float32
    )
    back_rows_norm, grad_gain_attn = norm_attn_back(back_normed)
    tokens_grad = (
        (back_resid + back_rows_norm).astype(jnp.bfloat16).reshape(layer_activations.shape)
    )
    local_grads = (grad_gain_attn, grad_qkv, grad_out, grad_gain_mix, grad_ctrl, grad_in, grad_down)
    summed = lax.psum(
        (
            local_grads[0],
            local_grads[1],
            local_grads[2],
            local_grads[3],
            local_grads[4],
            local_grads[5],
            local_grads[6],
        ),
        ("batch", "seq"),
    )
    return (
        block_out,
        tokens_grad,
        summed[0],
        summed[1],
        summed[2],
        summed[3],
        summed[4],
        summed[5],
        summed[6],
    )


def solution(mesh):
    placed = (
        P("batch", "seq", None),
        P("batch"),
        P("batch", "seq"),
        P(),
        P(),
        P(),
        P(),
        P(),
        P(),
        P(),
        P(),
        P("batch", "seq", None),
    )
    return jax.shard_map(
        body,
        mesh=mesh,
        in_specs=placed,
        out_specs=(
            P("batch", "seq", None),
            P("batch", "seq", None),
            P(),
            P(),
            P(),
            P(),
            P(),
            P(),
            P(),
        ),
        check_vma=False,
    )
```

profile of v0, /device:TPU:0, one launch (start us, length us, event | category | flops | bytes accessed | tf_op | source)
XLA Modules:
  0.0 1201.7 jit_solution(8671697195641459902)
XLA Ops:
  24.4 27.7 %all-gather.5.cloned.1.call-done = bf16[4096,512]{1,0:T(8,128)(2,1)} async-done(((bf16[1024,512]{1,0:T(8,128)(2,1)}), bf16[4096,512]{1,0:T(8,128)(2,1)}) %all-gather.5.cloned.1.call-update) | async-done | bytes 4194320 | tf_op jit(solution)/shard_map/all_gather | solution.py:140
  58.4 8.7 copy.74
  67.0 21.7 %all-gather.7.cloned.1.call-done = bf16[4096,512]{1,0:T(8,128)(2,1)} async-done(((bf16[1024,512]{1,0:T(8,128)(2,1)}), bf16[4096,512]{1,0:T(8,128)(2,1)}) %all-gather.7.cloned.1.call-update) | async-done | bytes 4194320 | tf_op jit(solution)/shard_map/all_gather | solution.py:141
  95.1 8.3 copy.75
  104.5 187.6 %while.30 = (s32[]{:T(128)}, bf16[8,1024,64]{1,2,0:T(8,128)(2,1)}, f32[8,1024]{1,0:T(8,128)S(1)}, f32[8,1024]{1,0:T(8,128)S(1)}, s32[8]{0:T(128)S(1)}, /*index=5...) while((s32[]{:T(128)}, bf16[8,1024,64]{1,2,0:T(8,128)(2,1)}, ...), condition=%wide.region_4.5_spmd.clone.clone, body=%wide.region_1.4_spmd.clone.clone.sunk | while | flops 1149242368 | bytes 53024912 | solution.py:153
  112.5 6.8 fusion.193
  119.4 8.8 fusion.194
  135.9 6.8 fusion.193
  142.7 8.8 fusion.194
  159.3 6.8 fusion.193
  166.1 8.8 fusion.194
  182.6 6.8 fusion.193
  189.5 8.8 fusion.194
  212.9 8.8 fusion.194
  229.4 6.8 fusion.193
  236.2 8.8 fusion.194
  252.8 6.8 fusion.193
  259.6 8.8 fusion.194
  276.1 6.8 fusion.193
  283.0 8.8 fusion.194
  311.8 400.3 %while.31 = (s32[]{:T(128)}, bf16[8,1024,64]{1,2,0:T(8,128)(2,1)}, f32[8,4096,128]{1,2,0:T(8,128)}, s32[8]{0:T(128)S(1)}, bf16[8,1024,64]{2,1,0:T(8,128)(2,1)}, ...) while((s32[]{:T(128)}, bf16[8,1024,64]{1,2,0:T(8,128)(2,1)}, ...), condition=%wide.region_19.20_spmd.clone.clone, body=%wide.region_17.19_spmd.clone.clone.sunk | while | flops 2735542272 | bytes 186961168 | solution.py:241
  312.0 9.4 fusion.203
  322.7 14.9 %multiply_reduce_fusion.5 = (f32[1024]{0:T(1024)S(1)}, f32[1024,4096]{1,0:T(8,128)}) fusion(f32[1024,4096]{1,0:T(8,128)} %fusion.203, f32[1024]{0:T(1024)S(1)} %bitcast.243, f32[1024]{0:T(1024)S(1)} %bitcast.244, bf16[8,4096,64]{2,1,0:T(8,128)(2,1)} %get-tuple-element.575, s32[]{:T(128)S(6)} %copy.126, bf16[8,1024,64]{2,1,0:T(8,128)(2,1)} %get-tuple-element.574, ...), kind=kOutput, calls=%fused_computation.29.clone.1 | convolution fusion | flops 570424320 | bytes 34886656 | tf_op jit(solution)/shard_map/while/body/eval_jaxpr/qd,kd->qk/dot_general | solution.py:57
  337.6 12.3 %multiply_convert_fusion.4 = bf16[1024,4096]{1,0:T(8,128)(2,1)S(1)} fusion(f32[1024,4096]{1,0:T(8,128)} %get-tuple-element.511, f32[1024,4096]{1,0:T(8,128)} %fusion.203, f32[1024]{0:T(1024)S(1)} %get-tuple-element.512), kind=kLoop, calls=%fused_computation.28.clone.1 | loop fusion | flops 12582912 | bytes 41947136 | tf_op jit(solution)/shard_map/while/body/eval_jaxpr/convert_element_type | solution.py:93
  362.0 9.4 fusion.203
  372.7 14.9 %multiply_reduce_fusion.5 = (f32[1024]{0:T(1024)S(1)}, f32[1024,4096]{1,0:T(8,128)}) fusion(f32[1024,4096]{1,0:T(8,128)} %fusion.203, f32[1024]{0:T(1024)S(1)} %bitcast.243, f32[1024]{0:T(1024)S(1)} %bitcast.244, bf16[8,4096,64]{2,1,0:T(8,128)(2,1)} %get-tuple-element.575, s32[]{:T(128)S(6)} %copy.126, bf16[8,1024,64]{2,1,0:T(8,128)(2,1)} %get-tuple-element.574, ...), kind=kOutput, calls=%fused_computation.29.clone.1 | convolution fusion | flops 570424320 | bytes 34886656 | tf_op jit(solution)/shard_map/while/body/eval_jaxpr/qd,kd->qk/dot_general | solution.py:57
  387.6 12.3 %multiply_convert_fusion.4 = bf16[1024,4096]{1,0:T(8,128)(2,1)S(1)} fusion(f32[1024,4096]{1,0:T(8,128)} %get-tuple-element.511, f32[1024,4096]{1,0:T(8,128)} %fusion.203, f32[1024]{0:T(1024)S(1)} %get-tuple-element.512), kind=kLoop, calls=%fused_computation.28.clone.1 | loop fusion | flops 12582912 | bytes 41947136 | tf_op jit(solution)/shard_map/while/body/eval_jaxpr/convert_element_type | solution.py:93
  412.0 9.4 fusion.203
  422.7 14.9 %multiply_reduce_fusion.5 = (f32[1024]{0:T(1024)S(1)}, f32[1024,4096]{1,0:T(8,128)}) fusion(f32[1024,4096]{1,0:T(8,128)} %fusion.203, f32[1024]{0:T(1024)S(1)} %bitcast.243, f32[1024]{0:T(1024)S(1)} %bitcast.244, bf16[8,4096,64]{2,1,0:T(8,128)(2,1)} %get-tuple-element.575, s32[]{:T(128)S(6)} %copy.126, bf16[8,1024,64]{2,1,0:T(8,128)(2,1)} %get-tuple-element.574, ...), kind=kOutput, calls=%fused_computation.29.clone.1 | convolution fusion | flops 570424320 | bytes 34886656 | tf_op jit(solution)/shard_map/while/body/eval_jaxpr/qd,kd->qk/dot_general | solution.py:57
  437.6 12.3 %multiply_convert_fusion.4 = bf16[1024,4096]{1,0:T(8,128)(2,1)S(1)} fusion(f32[1024,4096]{1,0:T(8,128)} %get-tuple-element.511, f32[1024,4096]{1,0:T(8,128)} %fusion.203, f32[1024]{0:T(1024)S(1)} %get-tuple-element.512), kind=kLoop, calls=%fused_computation.28.clone.1 | loop fusion | flops 12582912 | bytes 41947136 | tf_op jit(solution)/shard_map/while/body/eval_jaxpr/convert_element_type | solution.py:93
  462.0 9.4 fusion.203
  472.7 14.9 %multiply_reduce_fusion.5 = (f32[1024]{0:T(1024)S(1)}, f32[1024,4096]{1,0:T(8,128)}) fusion(f32[1024,4096]{1,0:T(8,128)} %fusion.203, f32[1024]{0:T(1024)S(1)} %bitcast.243, f32[1024]{0:T(1024)S(1)} %bitcast.244, bf16[8,4096,64]{2,1,0:T(8,128)(2,1)} %get-tuple-element.575, s32[]{:T(128)S(6)} %copy.126, bf16[8,1024,64]{2,1,0:T(8,128)(2,1)} %get-tuple-element.574, ...), kind=kOutput, calls=%fused_computation.29.clone.1 | convolution fusion | flops 570424320 | bytes 34886656 | tf_op jit(solution)/shard_map/while/body/eval_jaxpr/qd,kd->qk/dot_general | solution.py:57
  487.6 12.3 %multiply_convert_fusion.4 = bf16[1024,4096]{1,0:T(8,128)(2,1)S(1)} fusion(f32[1024,4096]{1,0:T(8,128)} %get-tuple-element.511, f32[1024,4096]{1,0:T(8,128)} %fusion.203, f32[1024]{0:T(1024)S(1)} %get-tuple-element.512), kind=kLoop, calls=%fused_computation.28.clone.1 | loop fusion | flops 12582912 | bytes 41947136 | tf_op jit(solution)/shard_map/while/body/eval_jaxpr/convert_element_type | solution.py:93
  512.1 9.4 fusion.203
  522.7 14.9 %multiply_reduce_fusion.5 = (f32[1024]{0:T(1024)S(1)}, f32[1024,4096]{1,0:T(8,128)}) fusion(f32[1024,4096]{1,0:T(8,128)} %fusion.203, f32[1024]{0:T(1024)S(1)} %bitcast.243, f32[1024]{0:T(1024)S(1)} %bitcast.244, bf16[8,4096,64]{2,1,0:T(8,128)(2,1)} %get-tuple-element.575, s32[]{:T(128)S(6)} %copy.126, bf16[8,1024,64]{2,1,0:T(8,128)(2,1)} %get-tuple-element.574, ...), kind=kOutput, calls=%fused_computation.29.clone.1 | convolution fusion | flops 570424320 | bytes 34886656 | tf_op jit(solution)/shard_map/while/body/eval_jaxpr/qd,kd->qk/dot_general | solution.py:57
  537.6 12.3 %multiply_convert_fusion.4 = bf16[1024,4096]{1,0:T(8,128)(2,1)S(1)} fusion(f32[1024,4096]{1,0:T(8,128)} %get-tuple-element.511, f32[1024,4096]{1,0:T(8,128)} %fusion.203, f32[1024]{0:T(1024)S(1)} %get-tuple-element.512), kind=kLoop, calls=%fused_computation.28.clone.1 | loop fusion | flops 12582912 | bytes 41947136 | tf_op jit(solution)/shard_map/while/body/eval_jaxpr/convert_element_type | solution.py:93
  562.1 9.4 fusion.203
  572.8 14.9 %multiply_reduce_fusion.5 = (f32[1024]{0:T(1024)S(1)}, f32[1024,4096]{1,0:T(8,128)}) fusion(f32[1024,4096]{1,0:T(8,128)} %fusion.203, f32[1024]{0:T(1024)S(1)} %bitcast.243, f32[1024]{0:T(1024)S(1)} %bitcast.244, bf16[8,4096,64]{2,1,0:T(8,128)(2,1)} %get-tuple-element.575, s32[]{:T(128)S(6)} %copy.126, bf16[8,1024,64]{2,1,0:T(8,128)(2,1)} %get-tuple-element.574, ...), kind=kOutput, calls=%fused_computation.29.clone.1 | convolution fusion | flops 570424320 | bytes 34886656 | tf_op jit(solution)/shard_map/while/body/eval_jaxpr/qd,kd->qk/dot_general | solution.py:57
  587.7 12.3 %multiply_convert_fusion.4 = bf16[1024,4096]{1,0:T(8,128)(2,1)S(1)} fusion(f32[1024,4096]{1,0:T(8,128)} %get-tuple-element.511, f32[1024,4096]{1,0:T(8,128)} %fusion.203, f32[1024]{0:T(1024)S(1)} %get-tuple-element.512), kind=kLoop, calls=%fused_computation.28.clone.1 | loop fusion | flops 12582912 | bytes 41947136 | tf_op jit(solution)/shard_map/while/body/eval_jaxpr/convert_element_type | solution.py:93
  612.1 9.4 fusion.203
  622.8 14.9 %multiply_reduce_fusion.5 = (f32[1024]{0:T(1024)S(1)}, f32[1024,4096]{1,0:T(8,128)}) fusion(f32[1024,4096]{1,0:T(8,128)} %fusion.203, f32[1024]{0:T(1024)S(1)} %bitcast.243, f32[1024]{0:T(1024)S(1)} %bitcast.244, bf16[8,4096,64]{2,1,0:T(8,128)(2,1)} %get-tuple-element.575, s32[]{:T(128)S(6)} %copy.126, bf16[8,1024,64]{2,1,0:T(8,128)(2,1)} %get-tuple-element.574, ...), kind=kOutput, calls=%fused_computation.29.clone.1 | convolution fusion | flops 570424320 | bytes 34886656 | tf_op jit(solution)/shard_map/while/body/eval_jaxpr/qd,kd->qk/dot_general | solution.py:57
  637.7 12.3 %multiply_convert_fusion.4 = bf16[1024,4096]{1,0:T(8,128)(2,1)S(1)} fusion(f32[1024,4096]{1,0:T(8,128)} %get-tuple-element.511, f32[1024,4096]{1,0:T(8,128)} %fusion.203, f32[1024]{0:T(1024)S(1)} %get-tuple-element.512), kind=kLoop, calls=%fused_computation.28.clone.1 | loop fusion | flops 12582912 | bytes 41947136 | tf_op jit(solution)/shard_map/while/body/eval_jaxpr/convert_element_type | solution.py:93
  662.1 9.4 fusion.203
  672.8 14.9 %multiply_reduce_fusion.5 = (f32[1024]{0:T(1024)S(1)}, f32[1024,4096]{1,0:T(8,128)}) fusion(f32[1024,4096]{1,0:T(8,128)} %fusion.203, f32[1024]{0:T(1024)S(1)} %bitcast.243, f32[1024]{0:T(1024)S(1)} %bitcast.244, bf16[8,4096,64]{2,1,0:T(8,128)(2,1)} %get-tuple-element.575, s32[]{:T(128)S(6)} %copy.126, bf16[8,1024,64]{2,1,0:T(8,128)(2,1)} %get-tuple-element.574, ...), kind=kOutput, calls=%fused_computation.29.clone.1 | convolution fusion | flops 570424320 | bytes 34886656 | tf_op jit(solution)/shard_map/while/body/eval_jaxpr/qd,kd->qk/dot_general | solution.py:57
  687.7 12.3 %multiply_convert_fusion.4 = bf16[1024,4096]{1,0:T(8,128)(2,1)S(1)} fusion(f32[1024,4096]{1,0:T(8,128)} %get-tuple-element.511, f32[1024,4096]{1,0:T(8,128)} %fusion.203, f32[1024]{0:T(1024)S(1)} %get-tuple-element.512), kind=kLoop, calls=%fused_computation.28.clone.1 | loop fusion | flops 12582912 | bytes 41947136 | tf_op jit(solution)/shard_map/while/body/eval_jaxpr/convert_element_type | solution.py:93
  728.5 109.9 %reduce-scatter.2.cloned.1.call-done = f32[1,8,1024,128]{2,3,1,0:T(8,128)} async-done(((f32[1,8,4096,128]{2,3,1,0:T(8,128)}), f32[1,8,1024,128]{2,3,1,0:T(8,128)}) %reduce-scatter.2.cloned.1.call-update) | async-done | bytes 4194320 | tf_op jit(solution)/shard_map/reduce_scatter | solution.py:246
  859.6 42.1 %all-reduce = (f32[512]{0:T(512)}, f32[512]{0:T(512)}, f32[512,2]{0,1:T(2,128)}) all-reduce(f32[512]{0:T(512)S(1)} %get-tuple-element.306, f32[512]{0:T(512)S(1)} %copy-done.47, f32[512,2]{0,1:T(2,128)S(1)} %fusion.135), channel_id=1, replica_groups=mesh['batch'=8,'seq'=4] {'batch','seq'}, use_global_device_ids=true, to_apply=%region_23.24 | all-reduce | flops 2048 | bytes 16384 | tf_op jit(solution)/shard_map/psum | solution.py:261
  901.6 277.8 %all-reduce.4.cloned.1.call-done = (f32[512,1536]{1,0:T(8,128)}, f32[512,512]{1,0:T(8,128)}, f32[2,512,2048]{2,1,0:T(8,128)}, f32[2,2048,512]{2,1,0:T(8,128)}) async-done(((f32[512,1536]{1,0:T(8,128)}, f32[512,512]{1,0:T(8,128)}, f32[2,512,2048]{2,1,0:T(8,128)}, f32[2,2048,512]{2,1,0:T(8,128)}), (f32[512,1536]{1,0:T(8,128)}, f32[512,512]{1,0:T(8,128)}, f32[2,512,2048]{2,1,0:T(8,128)}, ...) | async-done | bytes 20971536 | tf_op jit(solution)/shard_map/psum | solution.py:261
  (364 shorter events, 277.1 us)
Async XLA Ops:
  7.2 44.9 %all-gather.5.cloned.1.call-start = ((), (), s32[]{:S(2)}) async-start(), calls=%async_computation.2 | async-start | bytes 5242880 | tf_op jit(solution)/shard_map/all_gather | solution.py:140
  14.7 7.7 copy-start.11
  14.7 74.0 %all-gather.7.cloned.1.call-start = ((), (), s32[]{:S(2)}) async-start(), calls=%async_computation.3 | async-start | bytes 5242880 | tf_op jit(solution)/shard_map/all_gather | solution.py:141
  14.8 9.0 copy-start.48
  15.5 823.0 %reduce-scatter.2.cloned.1.call-start = ((), (), s32[]{:S(2)}) async-start(), calls=%async_computation.1 | async-start | bytes 20971520 | tf_op jit(solution)/shard_map/reduce_scatter | solution.py:246
  104.5 187.7 %copy-start.8 = (bf16[1,1024,512]{1,2,0:T(8,128)(2,1)S(1)}, bf16[1,1024,512]{1,2,0:T(8,128)(2,1)}, u32[]{:S(2)}) copy-start(bf16[1,1024,512]{1,2,0:T(8,128)(2,1)} %copy-done.7) | copy-start | bytes 3145732
  104.5 187.7 %copy-start.21 = (bf16[512,512]{1,0:T(8,128)(2,1)S(1)}, bf16[512,512]{1,0:T(8,128)(2,1)}, u32[]{:S(2)}) copy-start(bf16[512,512]{1,0:T(8,128)(2,1)} %param.22) | copy-start | bytes 1572868
  294.3 11.9 copy-start.1
  294.6 9.3 copy-start.4
  295.4 8.0 copy-start.33
  337.5 17.8 %slice-start = ((s8[16777216]{0:T(1024)(128)(4,1)}), s8[4194304]{0:T(1024)(128)(4,1)S(1)}, s32[]{:S(2)}) async-start(s8[16777216]{0:T(1024)(128)(4,1)} %bitcast.223), calls=%async_computation.5 | async-start | bytes 8388608 | tf_op jit(solution)/shard_map/while
  337.6 17.8 %slice-start.1 = ((s8[16777216]{0:T(1024)(128)(4,1)}), s8[4194304]{0:T(1024)(128)(4,1)S(1)}, s32[]{:S(2)}) async-start(s8[16777216]{0:T(1024)(128)(4,1)} %bitcast.223), calls=%async_computation.6 | async-start | bytes 8388608 | tf_op jit(solution)/shard_map/while
  337.6 17.8 %slice-start.2 = ((s8[16777216]{0:T(1024)(128)(4,1)}), s8[4194304]{0:T(1024)(128)(4,1)S(1)}, s32[]{:S(2)}) async-start(s8[16777216]{0:T(1024)(128)(4,1)} %bitcast.223), calls=%async_computation.7 | async-start | bytes 8388608 | tf_op jit(solution)/shard_map/while
  337.6 17.8 %slice-start.3 = ((s8[16777216]{0:T(1024)(128)(4,1)}), s8[4194304]{0:T(1024)(128)(4,1)S(1)}, s32[]{:S(2)}) async-start(s8[16777216]{0:T(1024)(128)(4,1)} %bitcast.223), calls=%async_computation.8 | async-start | bytes 8388608 | tf_op jit(solution)/shard_map/while
  387.6 17.8 %slice-start = ((s8[16777216]{0:T(1024)(128)(4,1)}), s8[4194304]{0:T(1024)(128)(4,1)S(1)}, s32[]{:S(2)}) async-start(s8[16777216]{0:T(1024)(128)(4,1)} %bitcast.223), calls=%async_computation.5 | async-start | bytes 8388608 | tf_op jit(solution)/shard_map/while
  387.6 17.8 %slice-start.1 = ((s8[16777216]{0:T(1024)(128)(4,1)}), s8[4194304]{0:T(1024)(128)(4,1)S(1)}, s32[]{:S(2)}) async-start(s8[16777216]{0:T(1024)(128)(4,1)} %bitcast.223), calls=%async_computation.6 | async-start | bytes 8388608 | tf_op jit(solution)/shard_map/while
  387.6 17.8 %slice-start.2 = ((s8[16777216]{0:T(1024)(128)(4,1)}), s8[4194304]{0:T(1024)(128)(4,1)S(1)}, s32[]{:S(2)}) async-start(s8[16777216]{0:T(1024)(128)(4,1)} %bitcast.223), calls=%async_computation.7 | async-start | bytes 8388608 | tf_op jit(solution)/shard_map/while
  387.6 17.8 %slice-start.3 = ((s8[16777216]{0:T(1024)(128)(4,1)}), s8[4194304]{0:T(1024)(128)(4,1)S(1)}, s32[]{:S(2)}) async-start(s8[16777216]{0:T(1024)(128)(4,1)} %bitcast.223), calls=%async_computation.8 | async-start | bytes 8388608 | tf_op jit(solution)/shard_map/while
  437.5 17.8 %slice-start = ((s8[16777216]{0:T(1024)(128)(4,1)}), s8[4194304]{0:T(1024)(128)(4,1)S(1)}, s32[]{:S(2)}) async-start(s8[16777216]{0:T(1024)(128)(4,1)} %bitcast.223), calls=%async_computation.5 | async-start | bytes 8388608 | tf_op jit(solution)/shard_map/while
  437.6 17.8 %slice-start.1 = ((s8[16777216]{0:T(1024)(128)(4,1)}), s8[4194304]{0:T(1024)(128)(4,1)S(1)}, s32[]{:S(2)}) async-start(s8[16777216]{0:T(1024)(128)(4,1)} %bitcast.223), calls=%async_computation.6 | async-start | bytes 8388608 | tf_op jit(solution)/shard_map/while
  437.6 17.8 %slice-start.2 = ((s8[16777216]{0:T(1024)(128)(4,1)}), s8[4194304]{0:T(1024)(128)(4,1)S(1)}, s32[]{:S(2)}) async-start(s8[16777216]{0:T(1024)(128)(4,1)} %bitcast.223), calls=%async_computation.7 | async-start | bytes 8388608 | tf_op jit(solution)/shard_map/while
  437.6 17.8 %slice-start.3 = ((s8[16777216]{0:T(1024)(128)(4,1)}), s8[4194304]{0:T(1024)(128)(4,1)S(1)}, s32[]{:S(2)}) async-start(s8[16777216]{0:T(1024)(128)(4,1)} %bitcast.223), calls=%async_computation.8 | async-start | bytes 8388608 | tf_op jit(solution)/shard_map/while
  487.6 17.8 %slice-start = ((s8[16777216]{0:T(1024)(128)(4,1)}), s8[4194304]{0:T(1024)(128)(4,1)S(1)}, s32[]{:S(2)}) async-start(s8[16777216]{0:T(1024)(128)(4,1)} %bitcast.223), calls=%async_computation.5 | async-start | bytes 8388608 | tf_op jit(solution)/shard_map/while
  487.6 17.8 %slice-start.1 = ((s8[16777216]{0:T(1024)(128)(4,1)}), s8[4194304]{0:T(1024)(128)(4,1)S(1)}, s32[]{:S(2)}) async-start(s8[16777216]{0:T(1024)(128)(4,1)} %bitcast.223), calls=%async_computation.6 | async-start | bytes 8388608 | tf_op jit(solution)/shard_map/while
  487.6 17.8 %slice-start.2 = ((s8[16777216]{0:T(1024)(128)(4,1)}), s8[4194304]{0:T(1024)(128)(4,1)S(1)}, s32[]{:S(2)}) async-start(s8[16777216]{0:T(1024)(128)(4,1)} %bitcast.223), calls=%async_computation.7 | async-start | bytes 8388608 | tf_op jit(solution)/shard_map/while
  487.6 17.8 %slice-start.3 = ((s8[16777216]{0:T(1024)(128)(4,1)}), s8[4194304]{0:T(1024)(128)(4,1)S(1)}, s32[]{:S(2)}) async-start(s8[16777216]{0:T(1024)(128)(4,1)} %bitcast.223), calls=%async_computation.8 | async-start | bytes 8388608 | tf_op jit(solution)/shard_map/while
  537.6 17.8 %slice-start = ((s8[16777216]{0:T(1024)(128)(4,1)}), s8[4194304]{0:T(1024)(128)(4,1)S(1)}, s32[]{:S(2)}) async-start(s8[16777216]{0:T(1024)(128)(4,1)} %bitcast.223), calls=%async_computation.5 | async-start | bytes 8388608 | tf_op jit(solution)/shard_map/while
  537.6 17.8 %slice-start.1 = ((s8[16777216]{0:T(1024)(128)(4,1)}), s8[4194304]{0:T(1024)(128)(4,1)S(1)}, s32[]{:S(2)}) async-start(s8[16777216]{0:T(1024)(128)(4,1)} %bitcast.223), calls=%async_computation.6 | async-start | bytes 8388608 | tf_op jit(solution)/shard_map/while
  537.6 17.8 %slice-start.2 = ((s8[16777216]{0:T(1024)(128)(4,1)}), s8[4194304]{0:T(1024)(128)(4,1)S(1)}, s32[]{:S(2)}) async-start(s8[16777216]{0:T(1024)(128)(4,1)} %bitcast.223), calls=%async_computation.7 | async-start | bytes 8388608 | tf_op jit(solution)/shard_map/while
  537.6 17.8 %slice-start.3 = ((s8[16777216]{0:T(1024)(128)(4,1)}), s8[4194304]{0:T(1024)(128)(4,1)S(1)}, s32[]{:S(2)}) async-start(s8[16777216]{0:T(1024)(128)(4,1)} %bitcast.223), calls=%async_computation.8 | async-start | bytes 8388608 | tf_op jit(solution)/shard_map/while
  587.6 17.8 %slice-start = ((s8[16777216]{0:T(1024)(128)(4,1)}), s8[4194304]{0:T(1024)(128)(4,1)S(1)}, s32[]{:S(2)}) async-start(s8[16777216]{0:T(1024)(128)(4,1)} %bitcast.223), calls=%async_computation.5 | async-start | bytes 8388608 | tf_op jit(solution)/shard_map/while
  587.6 17.8 %slice-start.1 = ((s8[16777216]{0:T(1024)(128)(4,1)}), s8[4194304]{0:T(1024)(128)(4,1)S(1)}, s32[]{:S(2)}) async-start(s8[16777216]{0:T(1024)(128)(4,1)} %bitcast.223), calls=%async_computation.6 | async-start | bytes 8388608 | tf_op jit(solution)/shard_map/while
  587.6 17.8 %slice-start.2 = ((s8[16777216]{0:T(1024)(128)(4,1)}), s8[4194304]{0:T(1024)(128)(4,1)S(1)}, s32[]{:S(2)}) async-start(s8[16777216]{0:T(1024)(128)(4,1)} %bitcast.223), calls=%async_computation.7 | async-start | bytes 8388608 | tf_op jit(solution)/shard_map/while
  587.6 17.8 %slice-start.3 = ((s8[16777216]{0:T(1024)(128)(4,1)}), s8[4194304]{0:T(1024)(128)(4,1)S(1)}, s32[]{:S(2)}) async-start(s8[16777216]{0:T(1024)(128)(4,1)} %bitcast.223), calls=%async_computation.8 | async-start | bytes 8388608 | tf_op jit(solution)/shard_map/while
  637.6 17.8 %slice-start = ((s8[16777216]{0:T(1024)(128)(4,1)}), s8[4194304]{0:T(1024)(128)(4,1)S(1)}, s32[]{:S(2)}) async-start(s8[16777216]{0:T(1024)(128)(4,1)} %bitcast.223), calls=%async_computation.5 | async-start | bytes 8388608 | tf_op jit(solution)/shard_map/while
  637.7 17.8 %slice-start.1 = ((s8[16777216]{0:T(1024)(128)(4,1)}), s8[4194304]{0:T(1024)(128)(4,1)S(1)}, s32[]{:S(2)}) async-start(s8[16777216]{0:T(1024)(128)(4,1)} %bitcast.223), calls=%async_computation.6 | async-start | bytes 8388608 | tf_op jit(solution)/shard_map/while
  637.7 17.8 %slice-start.2 = ((s8[16777216]{0:T(1024)(128)(4,1)}), s8[4194304]{0:T(1024)(128)(4,1)S(1)}, s32[]{:S(2)}) async-start(s8[16777216]{0:T(1024)(128)(4,1)} %bitcast.223), calls=%async_computation.7 | async-start | bytes 8388608 | tf_op jit(solution)/shard_map/while
  637.7 17.8 %slice-start.3 = ((s8[16777216]{0:T(1024)(128)(4,1)}), s8[4194304]{0:T(1024)(128)(4,1)S(1)}, s32[]{:S(2)}) async-start(s8[16777216]{0:T(1024)(128)(4,1)} %bitcast.223), calls=%async_computation.8 | async-start | bytes 8388608 | tf_op jit(solution)/shard_map/while
  687.7 17.8 %slice-start = ((s8[16777216]{0:T(1024)(128)(4,1)}), s8[4194304]{0:T(1024)(128)(4,1)S(1)}, s32[]{:S(2)}) async-start(s8[16777216]{0:T(1024)(128)(4,1)} %bitcast.223), calls=%async_computation.5 | async-start | bytes 8388608 | tf_op jit(solution)/shard_map/while
  687.7 17.8 %slice-start.1 = ((s8[16777216]{0:T(1024)(128)(4,1)}), s8[4194304]{0:T(1024)(128)(4,1)S(1)}, s32[]{:S(2)}) async-start(s8[16777216]{0:T(1024)(128)(4,1)} %bitcast.223), calls=%async_computation.6 | async-start | bytes 8388608 | tf_op jit(solution)/shard_map/while
  687.7 17.8 %slice-start.2 = ((s8[16777216]{0:T(1024)(128)(4,1)}), s8[4194304]{0:T(1024)(128)(4,1)S(1)}, s32[]{:S(2)}) async-start(s8[16777216]{0:T(1024)(128)(4,1)} %bitcast.223), calls=%async_computation.7 | async-start | bytes 8388608 | tf_op jit(solution)/shard_map/while
  687.7 17.8 %slice-start.3 = ((s8[16777216]{0:T(1024)(128)(4,1)}), s8[4194304]{0:T(1024)(128)(4,1)S(1)}, s32[]{:S(2)}) async-start(s8[16777216]{0:T(1024)(128)(4,1)} %bitcast.223), calls=%async_computation.8 | async-start | bytes 8388608 | tf_op jit(solution)/shard_map/while
  712.2 467.3 %all-reduce.4.cloned.1.call-start = ((), (), s32[]{:S(2)}) async-start(), calls=%async_computation.4 | async-start | bytes 41943040 | tf_op jit(solution)/shard_map/psum | solution.py:261
  728.5 114.1 %copy-start.9 = (bf16[1,1024,512]{1,2,0:T(8,128)(2,1)S(1)}, bf16[1,1024,512]{1,2,0:T(8,128)(2,1)}, u32[]{:S(2)}) copy-start(bf16[1,1024,512]{1,2,0:T(8,128)(2,1)} %copy-done.7) | copy-start | bytes 3145732
  728.5 114.1 %copy-start.43 = (f32[1024]{0:T(1024)S(1)}, f32[1024]{0:T(1024)}, u32[]{:S(2)}) copy-start(f32[1024]{0:T(1024)} %copy-done.42) | copy-start | bytes 12292
  728.5 114.1 %copy-start.46 = (f32[512]{0:T(512)S(1)}, f32[512]{0:T(512)}, u32[]{:S(2)}) copy-start(f32[512]{0:T(512)} %copy-done.45) | copy-start | bytes 6148
  1179.4 6.7 copy-start.14
  1183.3 7.0 slice-start.4
  (40 other events, 121.5 us)
Sparse Core Ops, SparseCore 0:
  14.8 37.1 all-gather.4
  54.2 34.4 all-gather.6
  712.3 126.1 reduce-scatter.1
  847.0 332.3 all-reduce.3
where the time goes:
time: 1210 us; the launch traced here: 1200 us
  matrix products  440 us (36%)
  waiting for transfers between devices  438 us (36%)
  other arithmetic  183 us (15%)
  local copies, waits for them, and re-layouts  81.3 us (7%)
  blocking collectives  42.1 us (3%)
  between operations  15.9 us (1%)
    psum x1, waiting for transfers between devices, body(): lax.psum((local_grads[0], local_grads[1], local_grads[2], local_grads[3],...  278 us
    dot_general x16, matrix products, head_probs(): jnp.einsum('qd,kd->qk', query_head, key_head, preferred_element_type=jnp....  169 us
    reduce_scatter x1, waiting for transfers between devices, body(): lax.psum_scatter(pair_grads, 'seq', scatter_dimension=2, tiled=True)  110 us
    convert_element_type x8, other arithmetic, attend_back(): (attn_probs * (back_probs - row_inner[:, None])).astype(jnp.bfloat16)  98.4 us
    dot_general x8, matrix products, attend_back(): jnp.einsum('qd,kd->qk', grad_head, value_head, preferred_element_type=jnp...  75.1 us
    dot_general x8, matrix products, attend_head(): jnp.einsum('qk,kd->qd', attn_probs.astype(jnp.bfloat16), value_head, pref...  70.3 us
    reduce_sum x8, other arithmetic, attend_head(): row_total = jnp.sum(raised, axis=1)  54.7 us
    unnamed x115, local copies, waits for them, and re-layouts  49.4 us
  transfers between devices with their start and end apart: 4, of which 4 were waited for; matrix products, arithmetic and copies ran while one was open for 4% of the time, Pallas kernels for 0%

commit v1 on v0

v1 whole, which is shorter than its diff:
```python
import jax
import jax.numpy as jnp
from jax import lax
from jax.experimental import pallas as pl
from jax.experimental.pallas import tpu as pltpu
from jax.sharding import PartitionSpec as P

HEADS = 8
HEAD = 64
GROUP = 32
EPSILON = 1e-06
LOG2E = 1.4426950408889634
SC = 0.125 * LOG2E
bf = jnp.bfloat16
f32 = jnp.float32
CORE = [(0, 1), (1, 0), (2, 3), (3, 2)]
CHIP = [(0, 2), (1, 3), (2, 0), (3, 1)]
UP = [(0, 2), (1, 3)]
DOWN = [(2, 0), (3, 1)]

BQ=512; NK=2048; NQ=2048
NT=(((1,),(1,)),((),()))
TN=(((0,),(0,)),((),()))
def row_iota(shape): return lax.broadcasted_iota(jnp.int32,shape,0)
def col_iota(shape): return lax.broadcasted_iota(jnp.int32,shape,1)

def scores(kv, q, s_ref, slot, kmax, q0, limit, causal, CH=512):
    mx=None
    for k0 in range(0,kmax,CH):
        s=lax.dot_general(kv[k0:k0+CH,:],q,NT,preferred_element_type=f32)
        if causal:
            if k0>=1024:
                kp=row_iota(s.shape)+k0
                s=jnp.where(kp<limit,s,-1e30)
            if k0+CH>q0:
                s=jnp.where(row_iota(s.shape)+(k0-q0)<=col_iota(s.shape),s,-1e30)
        s_ref[slot,k0:k0+CH,:]=s
        m=jnp.max(s,axis=0,keepdims=True)
        mx=m if mx is None else jnp.maximum(mx,m)
    return mx
def finish(vt, s_ref, slot, mx, kmax, p_ref, o_ref, st_ref, q0, i, CH=512):
    mc=mx*SC
    acc=None
    for k0 in range(0,kmax,CH):
        p=jnp.exp2(s_ref[slot,k0:k0+CH,:]*SC-mc).astype(bf)
        p_ref[0,i,k0:k0+CH,:]=p
        d=jnp.dot(vt[:,k0:k0+CH],p,preferred_element_type=f32)
        acc=d if acc is None else acc+d
    l=acc[0:1,:]
    o_ref[0,:,q0:q0+BQ]=(acc[64:128,:]*(1.0/l)).astype(bf)
    st_ref[0,0:1,q0:q0+BQ]=mc
    st_ref[0,1:2,q0:q0+BQ]=l
def local_fwd_kernel(lim_ref, q_ref, kv_ref, p_ref, o_ref, st_ref, s_ref, vt_ref):
    limit=lim_ref[0]
    kv=kv_ref[...]
    vt=kv.T
    vt_ref[...]=jnp.where(row_iota(vt.shape)<64,jnp.ones((),bf),vt)
    nb=NQ//BQ
    mxs=[None]*nb
    mxs[0]=scores(kv_ref,q_ref[0:BQ,:],s_ref,0,BQ,0,limit,True)
    for i in range(nb):
        if i+1<nb:
            mxs[i+1]=scores(kv_ref,q_ref[(i+1)*BQ:(i+2)*BQ,:],s_ref,(i+1)%2,(i+2)*BQ,(i+1)*BQ,limit,True)
        finish(vt_ref,s_ref,i%2,mxs[i],(i+1)*BQ,p_ref,o_ref,st_ref,i*BQ,i)
def local_fwd(lim, qkv, heads=4):
    return pl.pallas_call(local_fwd_kernel, grid=(heads,),
        in_specs=[pl.BlockSpec(memory_space=pltpu.SMEM),
                  pl.BlockSpec((NQ,128),lambda h:(0,2*h)),pl.BlockSpec((NK,128),lambda h:(0,2*h+1))],
        out_specs=[pl.BlockSpec((1,NQ//BQ,NK,BQ),lambda h:(h,0,0,0)),pl.BlockSpec((1,64,NQ),lambda h:(h,0,0)),pl.BlockSpec((1,8,NQ),lambda h:(h,0,0))],
        out_shape=[jax.ShapeDtypeStruct((heads,NQ//BQ,NK,BQ),bf),jax.ShapeDtypeStruct((heads,64,NQ),bf),jax.ShapeDtypeStruct((heads,8,NQ),f32)],
        scratch_shapes=[pltpu.VMEM((2,NK,BQ),f32),pltpu.VMEM((128,NK),bf)],
        compiler_params=pltpu.CompilerParams(vmem_limit_bytes=56*2**20))(lim,qkv,qkv)
def cross_fwd_kernel(q_ref, kv_ref, p_ref, o_ref, st_ref, s_ref, vt_ref):
    vt=kv_ref[...].T
    vt_ref[...]=jnp.where(row_iota(vt.shape)<64,jnp.ones((),bf),vt)
    nb=NQ//BQ
    mxs=[None]*nb
    mxs[0]=scores(kv_ref,q_ref[0:BQ,:],s_ref,0,NK,0,None,False)
    for i in range(nb):
        if i+1<nb:
            mxs[i+1]=scores(kv_ref,q_ref[(i+1)*BQ:(i+2)*BQ,:],s_ref,(i+1)%2,NK,(i+1)*BQ,None,False)
        finish(vt_ref,s_ref,i%2,mxs[i],NK,p_ref,o_ref,st_ref,i*BQ,i)
def cross_fwd(q, kv):
    return pl.pallas_call(cross_fwd_kernel, grid=(1,),
        in_specs=[pl.BlockSpec((NQ,128),lambda h:(0,0)),pl.BlockSpec((NK,128),lambda h:(0,0))],
        out_specs=[pl.BlockSpec((1,NQ//BQ,NK,BQ),lambda h:(h,0,0,0)),pl.BlockSpec((1,64,NQ),lambda h:(h,0,0)),pl.BlockSpec((1,8,NQ),lambda h:(h,0,0))],
        out_shape=[jax.ShapeDtypeStruct((1,NQ//BQ,NK,BQ),bf),jax.ShapeDtypeStruct((1,64,NQ),bf),jax.ShapeDtypeStruct((1,8,NQ),f32)],
        scratch_shapes=[pltpu.VMEM((2,NK,BQ),f32),pltpu.VMEM((128,NK),bf)],
        compiler_params=pltpu.CompilerParams(vmem_limit_bytes=56*2**20))(q,kv)

def bwd_block(kv_ref, kt_ref, q_ref, doT, delta, p_ref, i, kmax, q0, dkv_ref, dq_ref, CH=512, first=None):
    dob=doT.astype(bf)
    zer=jnp.zeros((64,BQ),bf)
    rhs=jnp.concatenate([zer,dob],axis=0)
    q=q_ref[q0:q0+BQ,:]
    dnat=rhs.T
    acc=None
    for k0 in range(0,kmax,CH):
        dp=jnp.dot(kv_ref[k0:k0+CH,:],rhs,preferred_element_type=f32)
        p=p_ref[0,i,k0:k0+CH,:]
        ds=(p.astype(f32)*(dp-delta)).astype(bf)
        d=jnp.dot(kt_ref[:,k0:k0+CH],ds,preferred_element_type=f32)
        acc=d if acc is None else acc+d
        g=jnp.dot(ds,q,preferred_element_type=f32)+jnp.dot(p,dnat,preferred_element_type=f32)
        isfirst = (i==0) if first is None else (k0>=first)
        if isfirst: dkv_ref[0,k0:k0+CH,:]=g
        else: dkv_ref[0,k0:k0+CH,:]+=g
    dq_ref[0,:,q0:q0+BQ]=(acc*0.125).astype(dq_ref.dtype)
def local_bwd_kernel(q_ref, kv_ref, p_ref, do_ref, st_ref, dkv_ref, dq_ref, kt_ref):
    kt_ref[...]=kv_ref[...].T[0:64,:]
    for i in range(NQ//BQ):
        q0=i*BQ
        r=st_ref[0,0:1,q0:q0+BQ]
        delta=st_ref[0,1:2,q0:q0+BQ]
        doT=do_ref[0,:,q0:q0+BQ].astype(f32)*r
        bwd_block(kv_ref,kt_ref,q_ref,doT,delta,p_ref,i,q0+BQ,q0,dkv_ref,dq_ref,first=q0)
def local_bwd(qkv,p,do,st,heads=4):
    return pl.pallas_call(local_bwd_kernel, grid=(heads,),
        in_specs=[pl.BlockSpec((NQ,128),lambda h:(0,2*h)),pl.BlockSpec((NK,128),lambda h:(0,2*h+1)),
                  pl.BlockSpec((1,NQ//BQ,NK,BQ),lambda h:(h,0,0,0)),pl.BlockSpec((1,64,NQ),lambda h:(h,0,0)),pl.BlockSpec((1,8,NQ),lambda h:(h,0,0))],
        out_specs=[pl.BlockSpec((1,NK,128),lambda h:(h,0,0)),pl.BlockSpec((1,64,NQ),lambda h:(h,0,0))],
        out_shape=[jax.ShapeDtypeStruct((heads,NK,128),f32),jax.ShapeDtypeStruct((heads,64,NQ),bf)],
        scratch_shapes=[pltpu.VMEM((64,NK),bf)],
        compiler_params=pltpu.CompilerParams(vmem_limit_bytes=56*2**20))(qkv,qkv,p,do,st)
def cross_bwd_kernel(q_ref, kv_ref, p_ref, do_ref, st_ref, dkv_ref, dq_ref, kt_ref):
    kt_ref[...]=kv_ref[...].T[0:64,:]
    for i in range(NQ//BQ):
        q0=i*BQ
        r=st_ref[0,0:1,q0:q0+BQ]
        delta=st_ref[0,1:2,q0:q0+BQ]
        doT=do_ref[0,:,q0:q0+BQ].astype(f32)*r
        bwd_block(kv_ref,kt_ref,q_ref,doT,delta,p_ref,i,NK,q0,dkv_ref,dq_ref)
def cross_bwd(q,kv,p,do,st):
    return pl.pallas_call(cross_bwd_kernel, grid=(1,),
        in_specs=[pl.BlockSpec((NQ,128),lambda h:(0,0)),pl.BlockSpec((NK,128),lambda h:(0,0)),
                  pl.BlockSpec((1,NQ//BQ,NK,BQ),lambda h:(h,0,0,0)),pl.BlockSpec((1,64,NQ),lambda h:(h,0,0)),pl.BlockSpec((1,8,NQ),lambda h:(h,0,0))],
        out_specs=[pl.BlockSpec((1,NK,128),lambda h:(h,0,0)),pl.BlockSpec((1,64,NQ),lambda h:(h,0,0))],
        out_shape=[jax.ShapeDtypeStruct((1,NK,128),f32),jax.ShapeDtypeStruct((1,64,NQ),bf)],
        scratch_shapes=[pltpu.VMEM((64,NK),bf)],
        compiler_params=pltpu.CompilerParams(vmem_limit_bytes=56*2**20))(q,kv,p,do,st)


def rms_norm(values, gain):
    inverse = lax.rsqrt(jnp.mean(values * values, axis=-1, keepdims=True) + EPSILON)
    return values * inverse * gain


def gelu_exact(values):
    return jax.nn.gelu(values, approximate=False)


def cluster_blend_shares(logit_vals, cluster_assignment):
    spread_mask = cluster_assignment[:, :, None]
    masked_vals = jnp.where(spread_mask, logit_vals[None, :, :], -jnp.inf)
    group_peak = jnp.max(masked_vals, axis=1)
    token_peak = jnp.sum(jnp.where(spread_mask, group_peak[:, None, :], 0.0), axis=0)
    raised = jnp.exp(logit_vals - token_peak)
    group_total = jnp.sum(jnp.where(spread_mask, raised[None, :, :], 0.0), axis=1)
    token_total = jnp.sum(jnp.where(spread_mask, group_total[:, None, :], 0.0), axis=0)
    return raised / token_total


def body(
    layer_activations,
    sequence_extents,
    position_cluster_label,
    cluster_sharpness,
    heed_scale_factor,
    triple_entry_matrix,
    heed_exit_matrix,
    blend_scale_factor,
    router_matrix,
    specialist_entry_matrix,
    specialist_exit_matrix,
    upstream_derivative,
):
    seq_count, pos_count, model_width = layer_activations.shape
    tok_count = seq_count * pos_count
    groups = tok_count // GROUP
    place = lax.axis_index("seq")
    chip = place // 2
    core = place % 2
    first = core == 0
    upper = chip == 1
    half = model_width // 2

    def ordered(mine, other, axis):
        return jnp.where(first, jnp.concatenate([mine, other], axis), jnp.concatenate([other, mine], axis))

    def pick(whole, own, axis):
        size = whole.shape[axis] // 2
        low = lax.slice_in_dim(whole, 0, size, axis=axis)
        high = lax.slice_in_dim(whole, size, 2 * size, axis=axis)
        return jnp.where(first == own, low, high)

    rows_low = layer_activations.reshape(tok_count, model_width)
    flat_rows = rows_low.astype(f32)
    pair_rows = ordered(rows_low, lax.ppermute(rows_low, "seq", CORE), 0).astype(f32)
    normed_attn, norm_attn_back = jax.vjp(rms_norm, flat_rows, heed_scale_factor.astype(f32))
    pair_normed = rms_norm(pair_rows, heed_scale_factor.astype(f32)).astype(bf)
    by_head = triple_entry_matrix.reshape(model_width, 3, HEADS, HEAD)
    own = lax.dynamic_slice_in_dim(by_head, core * 4, 4, axis=2)
    packed = jnp.stack([own[:, 0], jnp.zeros_like(own[:, 0]), own[:, 1], own[:, 2]], axis=2)
    packed = packed.reshape(model_width, 4 * 256)
    qkv = jnp.dot(pair_normed, packed, preferred_element_type=f32).astype(bf)
    payload = jnp.where(upper, jnp.concatenate([qkv[:, 512:576], qkv[:, 768:832]], 1), qkv[:, 128:256])
    got_a = lax.ppermute(payload, "seq", CHIP)
    got_b = lax.ppermute(qkv[:, 384:512], "seq", UP)
    limit = (sequence_extents - chip * 2 * pos_count).astype(jnp.int32)
    probs_near, out_near, stat_near = local_fwd(limit, qkv)
    blank = jnp.zeros((2 * pos_count, HEAD), bf)
    far_q, far_kv, far = [], [], []
    for j, got in ((0, got_a), (1, got_b)):
        far_q.append(jnp.where(upper, qkv[:, 256 * j : 256 * j + 128], jnp.concatenate([got_a[:, 64 * j : 64 * j + 64], blank], 1)))
        far_kv.append(jnp.where(upper, got, qkv[:, 256 * j + 640 : 256 * j + 768]))
        far.append(cross_fwd(far_q[j], far_kv[j]))
    out_far = jnp.concatenate([far[0][1], far[1][1]], 0)
    peak_far = jnp.concatenate([far[0][2], far[1][2]], 0)[:, 0]
    total_far = jnp.concatenate([far[0][2], far[1][2]], 0)[:, 1]
    log_far = peak_far + jnp.log2(total_far)
    got_out = lax.ppermute(out_far, "seq", UP)
    got_log = lax.ppermute(log_far, "seq", UP)
    peak_near, total_near = stat_near[:, 0], stat_near[:, 1]
    log_near = peak_near + jnp.log2(total_near)
    all_far = jnp.concatenate([out_far, got_out], 0)
    all_log = jnp.where(upper, jnp.concatenate([log_far, got_log], 0), -1e30)
    top = jnp.maximum(log_near, all_log)
    whole_log = top + jnp.log2(jnp.exp2(log_near - top) + jnp.exp2(all_log - top))
    share_near = jnp.exp2(log_near - whole_log)
    share_far = jnp.where(upper, jnp.exp2(all_log - whole_log), 0.0)
    joined = (out_near.astype(f32) * share_near[:, None, :] + jnp.where(upper, all_far.astype(f32), 0.0) * share_far[:, None, :]).astype(bf)
    flat_join = joined.reshape(half, 2 * pos_count)
    other_out = lax.ppermute(pick(flat_join, False, 1), "seq", CORE)
    attended_low = ordered(pick(flat_join, True, 1), other_out, 0).T
    branch = jnp.dot(attended_low, heed_exit_matrix, preferred_element_type=jnp.float32)
    resid = flat_rows + branch
    mix_normed, norm_mix_back = jax.vjp(rms_norm, resid, blend_scale_factor.astype(jnp.float32))
    mix_low = mix_normed.astype(jnp.bfloat16)
    logit_vals = jnp.dot(mix_low, router_matrix, preferred_element_type=jnp.float32)
    cluster_assignment = (
        position_cluster_label.reshape(tok_count)[None, :]
        == jnp.arange(groups, dtype=jnp.int32)[:, None]
    )

    def weigh(router_scores):
        return cluster_blend_shares(router_scores / cluster_sharpness[0], cluster_assignment)

    blend_coefficients, weigh_back = jax.vjp(weigh, logit_vals)
    weight_low = blend_coefficients.astype(jnp.bfloat16)
    mixing = jnp.where(
        cluster_assignment[None, :, :], weight_low.T[:, None, :], jnp.zeros((), jnp.bfloat16)
    )
    mixed_low = jnp.einsum(
        "egt,td->egd", mixing, mix_low, preferred_element_type=jnp.float32
    ).astype(jnp.bfloat16)
    inner = jnp.einsum(
        "egd,edh->egh", mixed_low, specialist_entry_matrix, preferred_element_type=jnp.float32
    )
    active, gelu_back = jax.vjp(gelu_exact, inner)
    active_low = active.astype(jnp.bfloat16)
    expert_low = jnp.einsum(
        "egh,ehd->egd", active_low, specialist_exit_matrix, preferred_element_type=jnp.float32
    ).astype(jnp.bfloat16)
    spread = jnp.einsum("egt,egd->td", mixing, expert_low, preferred_element_type=jnp.float32)
    block_out = (resid + spread).astype(jnp.bfloat16).reshape(layer_activations.shape)
    cot_low = upstream_derivative.reshape(tok_count, model_width)
    cot_full = cot_low.astype(jnp.float32)
    back_expert = jnp.einsum(
        "egt,td->egd", mixing, cot_low, preferred_element_type=jnp.float32
    ).astype(jnp.bfloat16)
    grad_down = jnp.einsum(
        "egh,egd->ehd", active_low, back_expert, preferred_element_type=jnp.float32
    )
    back_active = jnp.einsum(
        "egd,ehd->egh", back_expert, specialist_exit_matrix, preferred_element_type=jnp.float32
    )
    back_inner = gelu_back(back_active)[0].astype(jnp.bfloat16)
    grad_in = jnp.einsum("egd,egh->edh", mixed_low, back_inner, preferred_element_type=jnp.float32)
    back_mixed = jnp.einsum(
        "egh,edh->egd", back_inner, specialist_entry_matrix, preferred_element_type=jnp.float32
    ).astype(jnp.bfloat16)
    back_mixing = jnp.einsum("td,egd->egt", cot_low, expert_low, preferred_element_type=jnp.float32)
    back_mixing = back_mixing + jnp.einsum(
        "td,egd->egt", mix_low, back_mixed, preferred_element_type=jnp.float32
    )
    back_weight = jnp.sum(jnp.where(cluster_assignment[None, :, :], back_mixing, 0.0), axis=1).T
    back_logits = weigh_back(back_weight)[0].astype(jnp.bfloat16)
    grad_ctrl = jnp.einsum("td,te->de", mix_low, back_logits, preferred_element_type=jnp.float32)
    back_mix = jnp.einsum("egt,egd->td", mixing, back_mixed, preferred_element_type=jnp.float32)
    back_mix = back_mix + jnp.einsum(
        "te,de->td", back_logits, router_matrix, preferred_element_type=jnp.float32
    )
    back_resid_norm, grad_gain_mix = norm_mix_back(back_mix)
    back_resid = cot_full + back_resid_norm
    back_branch = back_resid.astype(jnp.bfloat16)
    grad_out = jnp.einsum(
        "td,te->de", attended_low, back_branch, preferred_element_type=jnp.float32
    )
    back_attended = jnp.einsum("de,te->dt", heed_exit_matrix, back_branch, preferred_element_type=f32).astype(bf)
    other_grad = lax.ppermute(pick(back_attended, False, 0), "seq", CORE)
    grads_out = ordered(pick(back_attended, True, 0), other_grad, 1).reshape(4, HEAD, 2 * pos_count)
    inner_rows = jnp.sum(grads_out.astype(f32) * joined.astype(f32), axis=1)
    got_grad = lax.ppermute(grads_out[2:4], "seq", DOWN)
    got_stat = lax.ppermute(jnp.stack([whole_log[2:4], inner_rows[2:4]]), "seq", DOWN)

    def scaled(peak, whole, inner):
        ratio = jnp.exp2(peak - whole)
        return jnp.stack([ratio, inner * ratio] + [jnp.zeros_like(ratio)] * 6, axis=1)

    near_kv, near_q = local_bwd(qkv, probs_near, grads_out, scaled(peak_near, whole_log, inner_rows))
    far_grad = jnp.where(upper, grads_out[0:2], got_grad)
    far_log = jnp.where(upper, whole_log[0:2], got_stat[0])
    far_inner = jnp.where(upper, inner_rows[0:2], got_stat[1])
    far_stat = scaled(peak_far, far_log, far_inner)
    far_back = [cross_bwd(far_q[j], far_kv[j], far[j][0], far_grad[j : j + 1], far_stat[j : j + 1]) for j in range(2)]
    far_kv_grad = jnp.concatenate([far_back[0][0], far_back[1][0]], 0)
    far_q_grad = jnp.concatenate([far_back[0][1], far_back[1][1]], 0)
    got_kv = lax.ppermute(far_kv_grad.astype(bf), "seq", DOWN)
    got_q = lax.ppermute(far_q_grad, "seq", UP)
    sum_q = near_q.astype(f32) + jnp.where(upper, jnp.concatenate([far_q_grad, got_q], 0).astype(f32), 0.0)
    sum_kv = near_kv + jnp.where(upper, 0.0, jnp.concatenate([got_kv.astype(f32), far_kv_grad], 0))
    sum_q = sum_q.astype(bf).reshape(half, 2 * pos_count).T
    sum_k = (sum_kv[:, :, :HEAD] * 0.125).astype(bf).transpose(1, 0, 2).reshape(2 * pos_count, half)
    sum_v = sum_kv[:, :, HEAD:].astype(bf).transpose(1, 0, 2).reshape(2 * pos_count, half)
    own_qkv = jnp.stack([sum_q, sum_k, sum_v], axis=1)
    own_grad = jnp.einsum("td,tjf->djf", pair_normed, own_qkv, preferred_element_type=f32)
    empty = jnp.zeros_like(own_grad)
    grad_qkv = ordered(own_grad, empty, 2).reshape(model_width, 3 * model_width)
    other_qkv = lax.ppermute(pick(own_qkv, False, 0), "seq", CORE)
    back_qkv = ordered(pick(own_qkv, True, 0), other_qkv, 2).reshape(tok_count, 3 * model_width)
    back_normed = jnp.einsum("tf,df->td", back_qkv, triple_entry_matrix, preferred_element_type=f32)
    back_rows_norm, grad_gain_attn = norm_attn_back(back_normed)
    tokens_grad = (
        (back_resid + back_rows_norm).astype(jnp.bfloat16).reshape(layer_activations.shape)
    )
    local_grads = (grad_gain_attn, grad_qkv, grad_out, grad_gain_mix, grad_ctrl, grad_in, grad_down)
    summed = lax.psum(
        (
            local_grads[0],
            local_grads[1],
            local_grads[2],
            local_grads[3],
            local_grads[4],
            local_grads[5],
            local_grads[6],
        ),
        ("batch", "seq"),
    )
    return (
        block_out,
        tokens_grad,
        summed[0],
        summed[1],
        summed[2],
        summed[3],
        summed[4],
        summed[5],
        summed[6],
    )


def solution(mesh):
    placed = (
        P("batch", "seq", None),
        P("batch"),
        P("batch", "seq"),
        P(),
        P(),
        P(),
        P(),
        P(),
        P(),
        P(),
        P(),
        P("batch", "seq", None),
    )
    return jax.shard_map(
        body,
        mesh=mesh,
        in_specs=placed,
        out_specs=(
            P("batch", "seq", None),
            P("batch", "seq", None),
            P(),
            P(),
            P(),
            P(),
            P(),
            P(),
            P(),
        ),
        check_vma=False,
    )
```

time: 1210 us -> 595 us (0.49)
  matrix products: 440 us -> 36.8 us
  other arithmetic: 183 us -> 31.6 us
  waiting for transfers between devices: 438 us -> 300 us
  Pallas kernels: 0 us -> 93.7 us
  local copies, waits for them, and re-layouts: 81.3 us -> 48.5 us
  starting transfers between devices: 0.41 us -> 16.4 us
    dot_general x59 -> x3, matrix products: 406 us -> 10 us  [the longest x1 5.07 us: body(): jnp.einsum('td,tjf->djf', pair_normed, own_qkv, preferred_element_type=f32)]
    reduce_scatter x1 -> x0, waiting for transfers between devices: 110 us -> none  [body(): lax.psum_scatter(pair_grads, 'seq', scatter_dimension=2, tiled=True)]
    convert_element_type x9 -> x4, other arithmetic: 99.1 us -> 4.37 us  [the longest x1 2.74 us: body(): sum_q = sum_q.astype(bf).reshape(half, 2 * pos_count).T]
    pallas_call x0 -> x6, Pallas kernels: none -> 93.7 us  [the longest x1 26.6 us: local_bwd(): pl.pallas_call(local_bwd_kernel, grid=(heads,), in_specs=[pl.BlockSpec((N...]
    reduce_sum x8 -> x1, other arithmetic: 54.7 us -> 1.51 us  [body(): inner_rows = jnp.sum(grads_out.astype(f32) * joined.astype(f32), axis=1)]
    all_gather x2 -> x0, waiting for transfers between devices: 49.4 us -> none  [the longest x1 27.7 us: body(): lax.all_gather(key_part, 'seq', axis=1, tiled=True)]
    ppermute x0 -> x12, waiting for transfers between devices: none -> 24.9 us  [the longest x1 11.4 us: body(): got_grad = lax.ppermute(grads_out[2:4], 'seq', DOWN)]
    unnamed x115 -> x109, local copies, waits for them, and re-layouts: 49.4 us -> 31.2 us
  transfers between devices with their start and end apart: 4 -> 13, of which waited for: 4 -> 5; matrix products, arithmetic and copies ran while one was open for 4% -> 6% of each run, Pallas kernels for 0% -> 8%
where the time goes in v1:
time: 595 us; the launch traced here: 587 us
  waiting for transfers between devices  300 us (50%)
  Pallas kernels  93.7 us (16%)
  local copies, waits for them, and re-layouts  48.5 us (8%)
  blocking collectives  43.6 us (7%)
  matrix products  36.8 us (6%)
  other arithmetic  31.6 us (5%)
  between operations  16.7 us (3%)
  starting transfers between devices  16.4 us (3%)
    psum x1, waiting for transfers between devices, body(): lax.psum((local_grads[0], local_grads[1], local_grads[2], local_grads[3],...  275 us
    psum x1, blocking collectives, body(): lax.psum((local_grads[0], local_grads[1], local_grads[2], local_grads[3],...  43.6 us
    unnamed x109, local copies, waits for them, and re-layouts  31.2 us
    pallas_call x1, Pallas kernels, local_bwd(): pl.pallas_call(local_bwd_kernel, grid=(heads,), in_specs=[pl.BlockSpec((N...  26.6 us
    pallas_call x2, Pallas kernels, cross_bwd(): pl.pallas_call(cross_bwd_kernel, grid=(1,), in_specs=[pl.BlockSpec((NQ, 1...  26 us
    pallas_call x2, Pallas kernels, cross_fwd(): pl.pallas_call(cross_fwd_kernel, grid=(1,), in_specs=[pl.BlockSpec((NQ, 1...  21.8 us
    pallas_call x1, Pallas kernels, local_fwd(): pl.pallas_call(local_fwd_kernel, grid=(heads,), in_specs=[pl.BlockSpec(me...  19.3 us
  transfers between devices with their start and end apart: 13, of which 5 were waited for; matrix products, arithmetic and copies ran while one was open for 6% of the time, Pallas kernels for 8%

profile of v1, /device:TPU:0, one launch (start us, length us, event | category | flops | bytes accessed | tf_op | source)
XLA Modules:
  0.0 587.4 jit_solution(13805243995173267607)
XLA Ops:
  7.2 1.5 copy.81
  9.3 1.7 copy.82
  11.7 2.4 fusion.2
  14.1 4.2 convolution_convert_fusion.q_ref.kv_ref
  19.0 1.4 copy-done.2
  20.4 2.9 collective-permute-start.1
  23.3 1.9 collective-permute-start.2
  25.9 19.3 %shard_map.190 = (bf16[4,4,2048,512]{3,2,1,0:T(8,128)(2,1)}, bf16[4,64,2048]{2,1,0:T(8,128)(2,1)}, f32[4,8,2048]{2,1,0:T(8,128)}) custom-call(s32[1]{0:T(128)S(6)} %sub.51.lim_ref, bf16[2048,1024]{1,0:T(8,128)(2,1)} %copy-done.2, bf16[2048,1024]{1,0:T(8,128)(2,1)} %copy-done.2), custom_call_target="tpu_custom_call" | custom-call | tf_op jit(solution)/shard_map/pallas_call | solution.py:66
  46.6 1.9 slice_select_fusion.2
  48.5 10.7 %shard_map.191 = (bf16[1,4,2048,512]{3,2,1,0:T(8,128)(2,1)}, bf16[1,64,2048]{2,1,0:T(8,128)(2,1)}, f32[1,8,2048]{2,1,0:T(8,128)}) custom-call(bf16[2048,128]{1,0:T(8,128)(2,1)} %get-tuple-element.97.q_ref, bf16[2048,128]{1,0:T(8,128)(2,1)} %get-tuple-element.96.kv_ref), custom_call_target="tpu_custom_call" | custom-call | tf_op jit(solution)/shard_map/pallas_call | solution.py:84
  60.1 11.1 %shard_map.192 = (bf16[1,4,2048,512]{3,2,1,0:T(8,128)(2,1)}, bf16[1,64,2048]{2,1,0:T(8,128)(2,1)}, f32[1,8,2048]{2,1,0:T(8,128)}) custom-call(bf16[2048,128]{1,0:T(8,128)(2,1)} %get-tuple-element.99.q_ref, bf16[2048,128]{1,0:T(8,128)(2,1)} %get-tuple-element.98.kv_ref), custom_call_target="tpu_custom_call" | custom-call | tf_op jit(solution)/shard_map/pallas_call | solution.py:84
  72.2 3.8 collective-permute-start.3
  78.6 10.5 %collective-permute-done.4 = bf16[2,64,2048]{2,1,0:T(8,128)(2,1)S(1)} collective-permute-done((bf16[2,64,2048]{2,1,0:T(8,128)(2,1)S(1)}, bf16[2,64,2048]{2,1,0:T(8,128)(2,1)S(1)}, u32[]{:S(2)}, u32[]{:S(2)}) %collective-permute-start.4) | collective-permute-done | bytes 524320 | tf_op jit(solution)/shard_map/ppermute | solution.py:221
  89.1 1.5 add_convert_fusion.1
  95.0 2.4 multiply_reduce_fusion.3
  102.2 1.7 add_convert_fusion.2
  104.0 1.3 convolution_convert_fusion.4
  105.3 4.6 fusion.127
  112.5 1.5 multiply_reduce_fusion
  116.0 2.9 fusion.34
  118.9 4.5 fusion.128
  123.4 1.5 multiply_reduce_fusion.1
  128.1 2.7 collective-permute-done.8
  131.7 11.4 %collective-permute-done.7 = bf16[2,64,2048]{2,1,0:T(8,128)(2,1)S(1)} collective-permute-done((bf16[2,64,2048]{2,1,0:T(8,128)(2,1)S(1)}, bf16[2,64,2048]{2,1,0:T(8,128)(2,1)S(1)}, u32[]{:S(2)}, u32[]{:S(2)}) %collective-permute-start.7) | collective-permute-done | bytes 524320 | tf_op jit(solution)/shard_map/ppermute | solution.py:303
  143.9 12.9 %shard_map.195 = (f32[1,2048,128]{2,1,0:T(8,128)}, bf16[1,64,2048]{2,1,0:T(8,128)(2,1)}) custom-call(bf16[2048,128]{1,0:T(8,128)(2,1)} %get-tuple-element.99.q_ref, bf16[2048,128]{1,0:T(8,128)(2,1)} %get-tuple-element.98.kv_ref, bf16[1,4,2048,512]{3,2,1,0:T(8,128)(2,1)} %get-tuple-element.34.p_ref, bf16[1,64,2048]{2,1,0:T(8,128)(2,1)} %get-tuple-element.116.do_ref, ...), custom_call_target="tpu_custom_call" | custom-call | tf_op jit(solution)/shard_map/pallas_call | solution.py:134
  158.1 13.1 %shard_map.194 = (f32[1,2048,128]{2,1,0:T(8,128)}, bf16[1,64,2048]{2,1,0:T(8,128)(2,1)}) custom-call(bf16[2048,128]{1,0:T(8,128)(2,1)} %get-tuple-element.97.q_ref, bf16[2048,128]{1,0:T(8,128)(2,1)} %get-tuple-element.96.kv_ref, bf16[1,4,2048,512]{3,2,1,0:T(8,128)(2,1)} %get-tuple-element.32.p_ref, bf16[1,64,2048]{2,1,0:T(8,128)(2,1)} %get-tuple-element.115.do_ref, ...), custom_call_target="tpu_custom_call" | custom-call | tf_op jit(solution)/shard_map/pallas_call | solution.py:134
  173.5 1.5 collective-permute-start.9
  177.3 26.6 %shard_map.193 = (f32[4,2048,128]{2,1,0:T(8,128)}, bf16[4,64,2048]{2,1,0:T(8,128)(2,1)}) custom-call(bf16[2048,1024]{1,0:T(8,128)(2,1)} %copy-done.2, bf16[2048,1024]{1,0:T(8,128)(2,1)} %copy-done.2, bf16[4,4,2048,512]{3,2,1,0:T(8,128)(2,1)} %get-tuple-element.30.p_ref, bf16[4,64,2048]{2,1,0:T(8,128)(2,1)} %get-tuple-element.86.do_ref, ...), custom_call_target="tpu_custom_call" | custom-call | tf_op jit(solution)/shard_map/pallas_call | solution.py:118
  203.9 2.7 add_convert_fusion
  208.6 1.9 fusion.15
  210.5 1.7 fusion.14
  212.2 2.7 copy.100
  214.9 2.7 copy.101
  217.6 5.1 fusion.16
  222.6 2.1 pad_select_fusion
  224.8 3.5 copy.105
  228.3 2.2 pad_maximum_fusion
  230.6 1.9 broadcast_select_fusion.1
  232.7 1.4 fusion.19
  234.2 2.4 copy.106
  237.0 3.3 maximum_select_fusion.1
  240.4 2.1 fusion.13
  243.1 1.3 copy.107
  244.4 43.6 %all-reduce.3 = (f32[512]{0:T(512)}, f32[512]{0:T(512)}, f32[512,2]{0,1:T(2,128)}) all-reduce(f32[512]{0:T(512)S(1)} %get-tuple-element.68, f32[512]{0:T(512)S(1)} %copy-done.39, f32[512,2]{0,1:T(2,128)S(1)} %fusion.111), channel_id=1, replica_groups=mesh['batch'=8,'seq'=4] {'batch','seq'}, use_global_device_ids=true, to_apply=%region_17.18 | all-reduce | flops 2048 | bytes 16384 | tf_op jit(solution)/shard_map/psum | solution.py:337
  288.0 275.2 %all-reduce.7.cloned.1.call-done = (f32[512,1536]{1,0:T(8,128)}, f32[512,512]{1,0:T(8,128)}, f32[2,512,2048]{2,1,0:T(8,128)}, f32[2,2048,512]{2,1,0:T(8,128)}) async-done(((f32[512,1536]{1,0:T(8,128)}, f32[512,512]{1,0:T(8,128)}, f32[2,512,2048]{2,1,0:T(8,128)}, f32[2,2048,512]{2,1,0:T(8,128)}), (f32[512,1536]{1,0:T(8,128)}, f32[512,512]{1,0:T(8,128)}, f32[2,512,2048]{2,1,0:T(8,128)}, ...) | async-done | bytes 20971536 | tf_op jit(solution)/shard_map/psum | solution.py:337
  563.3 3.8 copy.131
  568.1 8.6 %copy.133 = f32[2,512,2048]{2,1,0:T(8,128)} copy(f32[2,512,2048]{2,1,0:T(8,128)} %get-tuple-element.133) | data formatting | bytes 16777216
  576.7 3.4 copy.134
  (198 shorter events, 35.5 us)
Async XLA Ops:
  7.2 87.8 %copy-start = (bf16[512,512]{1,0:T(8,128)(2,1)S(1)}, bf16[512,512]{1,0:T(8,128)(2,1)}, u32[]{:S(2)}) copy-start(bf16[512,512]{1,0:T(8,128)(2,1)} %param.18) | copy-start | bytes 1572868
  7.2 556.1 %all-reduce.7.cloned.1.call-start = ((), (), s32[]{:S(2)}) async-start(), calls=%async_computation | async-start | bytes 41943040 | tf_op jit(solution)/shard_map/psum | solution.py:337
  8.8 5.3 copy-start.9
  8.8 2.9 collective-permute-start
  9.3 4.8 copy-start.37
  14.1 4.2 copy-start.40
  20.4 25.9 %collective-permute-start.1 = (bf16[2048,128]{1,0:T(8,128)(2,1)S(1)}, bf16[2048,128]{1,0:T(8,128)(2,1)S(1)}, u32[]{:S(2)}, u32[]{:S(2)}) collective-permute-start(bf16[2048,128]{1,0:T(8,128)(2,1)S(1)} %get-tuple-element.101), channel_id=1, source_target_pairs={{0,2},{1,3},{2,0},{3,1},{4,6},{5,7},{6,4},{7,5},{8,10},{9,11},{10,... | collective-permute-start | bytes 1572872 | tf_op jit(solution)/shard_map/ppermute | solution.py:207
  23.3 23.3 %collective-permute-start.2 = (bf16[2048,128]{1,0:T(8,128)(2,1)S(1)}, bf16[2048,128]{1,0:T(8,128)(2,1)S(1)}, u32[]{:S(2)}, u32[]{:S(2)}) collective-permute-start(bf16[2048,128]{1,0:T(8,128)(2,1)S(1)} %get-tuple-element.100), channel_id=1, source_target_pairs={{0,2},{1,3},{4,6},{5,7},{8,10},{9,11},{12,14},{13,15},{16,18},{17,... | collective-permute-start | bytes 1572872 | tf_op jit(solution)/shard_map/ppermute | solution.py:208
  25.9 20.7 %copy-start.3 = (bf16[2048,1024]{1,0:T(8,128)(2,1)S(1)}, bf16[2048,1024]{1,0:T(8,128)(2,1)}, u32[]{:S(2)}) copy-start(bf16[2048,1024]{1,0:T(8,128)(2,1)} %copy-done.2) | copy-start | bytes 12582916
  25.9 20.7 %copy-start.47 = (pred[128]{0:T(512)(128)(4,1)S(1)}, pred[128]{0:T(512)(128)(4,1)}, u32[]{:S(2)}) copy-start(pred[128]{0:T(512)(128)(4,1)} %constant.63.clone.1) | copy-start | bytes 388
  48.5 40.5 %copy-start.24 = (bf16[4,64,2048]{2,1,0:T(8,128)(2,1)S(1)}, bf16[4,64,2048]{2,1,0:T(8,128)(2,1)}, u32[]{:S(2)}) copy-start(bf16[4,64,2048]{2,1,0:T(8,128)(2,1)} %get-tuple-element.24) | copy-start | bytes 3145732
  59.2 29.8 %copy-start.27 = (bf16[1,64,2048]{2,1,0:T(8,128)(2,1)S(1)}, bf16[1,64,2048]{2,1,0:T(8,128)(2,1)}, u32[]{:S(2)}) copy-start(bf16[1,64,2048]{2,1,0:T(8,128)(2,1)} %get-tuple-element.28) | copy-start | bytes 786436
  72.2 6.2 %collective-permute-start.3 = (f32[2,2048]{1,0:T(2,128)S(1)}, f32[2,2048]{1,0:T(2,128)S(1)}, u32[]{:S(2)}, u32[]{:S(2)}) collective-permute-start(f32[2,2048]{1,0:T(2,128)S(1)} %bitcast_add_fusion.2), channel_id=1, source_target_pairs={{0,2},{1,3},{4,6},{5,7},{8,10},{9,11},{12,14},{13,15},{16,18},{17,... | collective-permute-start | bytes 49160 | tf_op jit(solution)/shard_map/ppermute | solution.py:222
  77.1 11.9 %collective-permute-start.4 = (bf16[2,64,2048]{2,1,0:T(8,128)(2,1)S(1)}, bf16[2,64,2048]{2,1,0:T(8,128)(2,1)S(1)}, u32[]{:S(2)}, u32[]{:S(2)}) collective-permute-start(bf16[2,64,2048]{2,1,0:T(8,128)(2,1)S(1)} %pad_maximum_fusion.3), channel_id=1, source_target_pairs={{0,2},{1,3},{4,6},{5,7},{8,10},{9,11},{12,14},{13,15},{16,18},{17,... | collective-permute-start | bytes 1572872 | tf_op jit(solution)/shard_map/ppermute | solution.py:221
  89.0 2.6 copy-start.42
  89.0 4.5 copy-start.46
  89.0 4.5 copy-start.12
  91.6 3.4 collective-permute-start.5
  93.6 3.9 copy-start.34
  95.0 3.9 copy-start.13
  97.5 2.6 copy-start.8
  97.7 14.0 %copy-start.4 = (bf16[1024,512]{0,1:T(8,128)(2,1)}, bf16[1024,512]{0,1:T(8,128)(2,1)S(1)}, u32[]{:S(2)}) copy-start(bf16[1024,512]{0,1:T(8,128)(2,1)S(1)} %multiply_convert_fusion) | copy-start | bytes 3145732
  98.9 12.3 %copy-start.28 = (bf16[2,1024]{1,0:T(2,128)(2,1)}, bf16[2,1024]{1,0:T(2,128)(2,1)S(1)}, u32[]{:S(2)}) copy-start(bf16[2,1024]{1,0:T(2,128)(2,1)S(1)} %fusion.100) | copy-start | bytes 12292
  100.0 2.2 copy-start.20
  115.4 8.0 %collective-permute-start.6 = (bf16[256,1024]{1,0:T(8,128)(2,1)S(1)}, bf16[256,1024]{1,0:T(8,128)(2,1)S(1)}, u32[]{:S(2)}, u32[]{:S(2)}) collective-permute-start(bf16[256,1024]{1,0:T(8,128)(2,1)S(1)} %get-tuple-element.111), channel_id=1, source_target_pairs={{0,1},{1,0},{2,3},{3,2},{4,5},{5,4},{6,7},{7,6},{8,9},{9,8},{10,11... | collective-permute-start | bytes 1572872 | tf_op jit(solution)/shard_map/ppermute | solution.py:300
  118.9 4.5 copy-start.15
  125.0 5.9 %copy-start.43 = (f32[8]{0:T(128)S(1)}, f32[8]{0:T(128)}, u32[]{:S(2)}) copy-start(f32[8]{0:T(128)} %pad.36.clone) | copy-start | bytes 100
  125.0 5.9 %copy-start.44 = (f32[8]{0:T(128)S(1)}, f32[8]{0:T(128)}, u32[]{:S(2)}) copy-start(f32[8]{0:T(128)} %pad.35.clone) | copy-start | bytes 100
  125.0 5.8 collective-permute-start.8
  126.8 16.3 %collective-permute-start.7 = (bf16[2,64,2048]{2,1,0:T(8,128)(2,1)S(1)}, bf16[2,64,2048]{2,1,0:T(8,128)(2,1)S(1)}, u32[]{:S(2)}, u32[]{:S(2)}) collective-permute-start(bf16[2,64,2048]{2,1,0:T(8,128)(2,1)S(1)} %bitcast.190), channel_id=1, source_target_pairs={{2,0},{3,1},{6,4},{7,5},{10,8},{11,9},{14,12},{15,13},{18,16},{19,... | collective-permute-start | bytes 1572872 | tf_op jit(solution)/shard_map/ppermute | solution.py:303
  158.0 14.4 %copy-start.25 = (bf16[1,64,2048]{2,1,0:T(8,128)(2,1)S(1)}, bf16[1,64,2048]{2,1,0:T(8,128)(2,1)}, u32[]{:S(2)}) copy-start(bf16[1,64,2048]{2,1,0:T(8,128)(2,1)} %get-tuple-element.35) | copy-start | bytes 786436
  173.5 30.4 %collective-permute-start.9 = (bf16[2,64,2048]{2,1,0:T(8,128)(2,1)S(1)}, bf16[2,64,2048]{2,1,0:T(8,128)(2,1)S(1)}, u32[]{:S(2)}, u32[]{:S(2)}) collective-permute-start(bf16[2,64,2048]{2,1,0:T(8,128)(2,1)S(1)} %pad_maximum_fusion.4), channel_id=1, source_target_pairs={{0,2},{1,3},{4,6},{5,7},{8,10},{9,11},{12,14},{13,15},{16,18},{17,... | collective-permute-start | bytes 1572872 | tf_op jit(solution)/shard_map/ppermute | solution.py:319
  175.1 31.5 %collective-permute-start.10 = (bf16[2,2048,128]{2,1,0:T(8,128)(2,1)S(1)}, bf16[2,2048,128]{2,1,0:T(8,128)(2,1)S(1)}, u32[]{:S(2)}, u32[]{:S(2)}) collective-permute-start(bf16[2,2048,128]{2,1,0:T(8,128)(2,1)S(1)} %pad_maximum_fusion.2), channel_id=1, source_target_pairs={{2,0},{3,1},{6,4},{7,5},{10,8},{11,9},{14,12},{15,13},{18,16},{19,... | collective-permute-start | bytes 3145736 | tf_op jit(solution)/shard_map/ppermute | solution.py:318
  177.3 26.6 %copy-start.26 = (bf16[1,64,2048]{2,1,0:T(8,128)(2,1)S(1)}, bf16[1,64,2048]{2,1,0:T(8,128)(2,1)}, u32[]{:S(2)}) copy-start(bf16[1,64,2048]{2,1,0:T(8,128)(2,1)} %get-tuple-element.33) | copy-start | bytes 786436
  203.9 2.9 copy-start.21
  214.9 2.7 copy-start.38
  214.9 2.7 copy-start.41
  232.4 4.6 collective-permute-start.11
  232.7 3.9 copy-start.31
  232.7 3.9 copy-start.33
  234.2 2.4 copy-start.5
  234.2 2.8 copy-start.16
  237.0 3.4 copy-start.11
  237.0 3.4 copy-start.22
  563.3 3.8 copy-start.23
  567.1 9.5 %slice-start = ((s8[8388608]{0:T(1024)(128)(4,1)}), s8[4194304]{0:T(1024)(128)(4,1)S(1)}, s32[]{:S(2)}) async-start(s8[8388608]{0:T(1024)(128)(4,1)} %bitcast.176), calls=%async_computation.1 | async-start | bytes 8388608
  568.1 8.6 %slice-start.1 = ((s8[8388608]{0:T(1024)(128)(4,1)}), s8[4194304]{0:T(1024)(128)(4,1)S(1)}, s32[]{:S(2)}) async-start(s8[8388608]{0:T(1024)(128)(4,1)} %bitcast.176), calls=%async_computation.2 | async-start | bytes 8388608
  576.7 3.4 copy-start.1
  (15 other events, 23.6 us)
Sparse Core Ops, SparseCore 0:
  228.5 334.7 all-reduce.6
